TPU v7x, 128 devices: a whole 4x4x4 slice. The times are simulated.
128 devices in a mesh: ctx: 64 (over x_lo, y, z, core), fsdp: 2 (over x_hi).
Axes of the slice: x: 4 (x_hi: 2, x_lo: 2; x = x_hi * 2 + x_lo), y: 4, z: 4, core: 2. Of those that a mesh axis runs over, the one named last changes fastest.
Arguments:
- layer_input: bfloat16 [2, 8192, 1024], P('fsdp', 'ctx'), may hold values from -6 to 6
- positions: int32 [2, 8192], P('fsdp', 'ctx'), may hold values from 0 to 16383, as said below
- routes: int32 [2, 8192, 8], P('fsdp', 'ctx'), may hold values from 0 to 31, all different within a row; in each aligned block of 128 rows (0 to 127, 128 to 255, ..., all dimensions but the last counted through in order) at most 48 rows name the same one
- attn_gain: float32 [1024], replicated, may hold values from 0.1 to 1.9
- w_query: bfloat16 [1024, 1024], P(('ctx', 'fsdp')), may hold values from -0.1875 to 0.1875
- w_key: bfloat16 [1024, 512], P(('ctx', 'fsdp')), may hold values from -0.1875 to 0.1875
- w_value: bfloat16 [1024, 512], P(('ctx', 'fsdp')), may hold values from -0.1875 to 0.1875
- query_gain: float32 [64], replicated, may hold values from 0.1 to 1.9
- key_gain: float32 [64], replicated, may hold values from 0.1 to 1.9
- w_output: bfloat16 [1024, 1024], P(('ctx', 'fsdp')), may hold values from -6 to 6
- ffn_gain: float32 [1024], replicated, may hold values from 0.1 to 1.9
- w_router: bfloat16 [1024, 32], P(('ctx', 'fsdp')), may hold values from -0.09375 to 0.09375
- w_gate: bfloat16 [64, 1024, 256], P('ctx', None, 'fsdp'), may hold values from -0.1875 to 0.1875
- w_up: bfloat16 [64, 1024, 256], P('ctx', None, 'fsdp'), may hold values from -0.1875 to 0.1875
- w_down: bfloat16 [64, 256, 1024], P('ctx', 'fsdp'), may hold values from -4 to 4
- cotangent: bfloat16 [2, 8192, 1024], P('fsdp', 'ctx'), may hold values from -6 to 6
Outputs:
- layer_output: bfloat16 [2, 8192, 1024], P('fsdp', 'ctx')
- grad_input: float32 [2, 8192, 1024], P('fsdp', 'ctx')
- grad_attn_gain: float32 [1024], P(('ctx', 'fsdp'))
- grad_query: float32 [1024, 1024], P(('ctx', 'fsdp'))
- grad_key: float32 [1024, 512], P(('ctx', 'fsdp'))
- grad_value: float32 [1024, 512], P(('ctx', 'fsdp'))
- grad_query_gain: float32 [64], replicated
- grad_key_gain: float32 [64], replicated
- grad_output: float32 [1024, 1024], P(('ctx', 'fsdp'))
- grad_ffn_gain: float32 [1024], P(('ctx', 'fsdp'))
- grad_router: float32 [1024, 32], P(('ctx', 'fsdp'))
- grad_gate: float32 [64, 1024, 256], P('ctx', None, 'fsdp')
- grad_up: float32 [64, 1024, 256], P('ctx', None, 'fsdp')
- grad_down: float32 [64, 256, 1024], P('ctx', 'fsdp')
Inputs may be any that keep to these rules, and one draw needn't show every extreme that they name: Within each sequence positions strictly increase; the first is 0 and the last is 16383. `routes`: A token's 8 experts differ. Among the 128 tokens of one device, no expert is named by more than 48 of them.
All inputs are finite; a program needn't handle non-finite values.
Results may differ from a plain program's by a relative error of at most 0.023.
Values may be sent and summed in bfloat16 or wider, within the bound.
A program may use at most 256 MiB of HBM per device.

v0:
```python
import jax
import jax.numpy as jnp
from jax import lax
from jax.sharding import PartitionSpec as P

EPS = 1e-06
HIGH = lax.Precision.HIGHEST


def norm_stats(values_in):
    factor = lax.rsqrt(jnp.mean(values_in * values_in, axis=-1, keepdims=True) + EPS)
    return (values_in * factor, factor)


def norm_back(grad_normed, normed, factor):
    return factor * (grad_normed - normed * jnp.mean(grad_normed * normed, axis=-1, keepdims=True))


def rotate(vector, cosine, sine):
    half = vector.shape[-1] // 2
    first = vector[..., :half]
    second = vector[..., half:]
    return jnp.concatenate(
        [first * cosine - second * sine, second * cosine + first * sine], axis=-1
    )


def rotate_back(vector, cosine, sine):
    half = vector.shape[-1] // 2
    first = vector[..., :half]
    second = vector[..., half:]
    return jnp.concatenate(
        [first * cosine + second * sine, second * cosine - first * sine], axis=-1
    )


def rope_tables(positions, head_dim):
    steps = jnp.arange(head_dim // 2, dtype=jnp.float32) * (2.0 / head_dim)
    inverse = jnp.power(50000.0, -steps)
    angles = positions.astype(jnp.float32)[..., None] * inverse
    return (jnp.cos(angles), jnp.sin(angles))


def matmul(left, right):
    return jnp.dot(left, right, preferred_element_type=jnp.float32)


def matmul_tn(left, right):
    return lax.dot_general(
        left, right, (((0,), (0,)), ((), ())), preferred_element_type=jnp.float32
    )


def matmul_nt(left, right):
    return lax.dot_general(
        left, right, (((1,), (1,)), ((), ())), preferred_element_type=jnp.float32
    )


def local(
    layer_input,
    positions,
    routes,
    attn_gain,
    w_query,
    w_key,
    w_value,
    query_gain,
    key_gain,
    w_output,
    ffn_gain,
    w_router,
    w_gate,
    w_up,
    w_down,
    cotangent,
):
    tokens = layer_input.shape[1]
    width = layer_input.shape[2]
    head_dim = query_gain.shape[0]
    heads = width // head_dim
    kv_width = w_key.shape[1]
    kv_heads = kv_width // head_dim
    share = heads // kv_heads
    fanout = routes.shape[2]
    experts = w_router.shape[1]
    groups = lax.axis_size("ctx")
    capacity = min(tokens, max(2, 3 * tokens * fanout // (2 * experts)))
    slot_count = experts * capacity
    scale = head_dim ** (-0.5)
    gathered = (
        lax.all_gather(w_query, ("ctx", "fsdp"), axis=0, tiled=True),
        lax.all_gather(w_key, ("ctx", "fsdp"), axis=0, tiled=True),
        lax.all_gather(w_value, ("ctx", "fsdp"), axis=0, tiled=True),
        lax.all_gather(w_output, ("ctx", "fsdp"), axis=0, tiled=True),
        lax.all_gather(w_router, ("ctx", "fsdp"), axis=0, tiled=True),
    )
    query_full, key_full, value_full, output_full, router_full = gathered
    input_f = layer_input[0].astype(jnp.float32)
    normed_a, factor_a = norm_stats(input_f)
    normed_in = (normed_a * attn_gain).astype(jnp.bfloat16)
    query_raw = matmul(normed_in, query_full).reshape(tokens, heads, head_dim)
    key_raw = matmul(normed_in, key_full).reshape(tokens, kv_heads, head_dim)
    values_own = matmul(normed_in, value_full).astype(jnp.bfloat16)
    cosine, sine = rope_tables(positions[0], head_dim)
    cosine = cosine[:, None, :]
    sine = sine[:, None, :]
    normed_q, factor_q = norm_stats(query_raw)
    normed_k, factor_k = norm_stats(key_raw)
    queries = rotate(normed_q * query_gain, cosine, sine).astype(jnp.bfloat16)
    keys_own = rotate(normed_k * key_gain, cosine, sine).astype(jnp.bfloat16)
    keys_all, values_all = (
        lax.all_gather(keys_own.reshape(tokens, kv_width), "ctx", axis=0, tiled=True),
        lax.all_gather(values_own, "ctx", axis=0, tiled=True),
    )
    length = keys_all.shape[0]
    keys_heads = keys_all.reshape(length, kv_heads, head_dim).transpose(1, 0, 2)
    values_heads = values_all.reshape(length, kv_heads, head_dim).transpose(1, 0, 2)
    query_groups = queries.reshape(tokens, kv_heads, share, head_dim).transpose(1, 0, 2, 3)

    def forward_group(parts):
        query_part, key_part, value_part = parts
        scores = (
            jnp.einsum("qgd,kd->gqk", query_part, key_part, preferred_element_type=jnp.float32)
            * scale
        )
        peak = jnp.max(scores, axis=-1, keepdims=True)
        expo = jnp.exp(scores - peak)
        total = jnp.sum(expo, axis=-1, keepdims=True)
        probs_low = (expo / total).astype(jnp.bfloat16)
        mixed_part = jnp.einsum(
            "gqk,kd->qgd", probs_low, value_part, preferred_element_type=jnp.float32
        )
        return (mixed_part, peak + jnp.log(total))

    mixed_groups, log_totals = lax.map(forward_group, (query_groups, keys_heads, values_heads))
    attended = mixed_groups.transpose(1, 0, 2, 3).reshape(tokens, width).astype(jnp.bfloat16)
    residual = input_f + matmul(attended, output_full)
    normed_m, factor_m = norm_stats(residual)
    normed_mid = (normed_m * ffn_gain).astype(jnp.bfloat16)
    logits = matmul(normed_mid, router_full)
    router_peak = jnp.max(logits, axis=-1, keepdims=True)
    router_expo = jnp.exp(logits - router_peak)
    router_probs = router_expo / jnp.sum(router_expo, axis=-1, keepdims=True)
    chosen = routes[0][:, :, None] == jnp.arange(experts, dtype=jnp.int32)[None, None, :]
    gates = jnp.sum(jnp.where(chosen, router_probs[:, None, :], 0.0), axis=-1)
    flat_hits = chosen.reshape(tokens * fanout, experts).astype(jnp.int32)
    earlier = jnp.sum((jnp.cumsum(flat_hits, axis=0) - flat_hits) * flat_hits, axis=-1)
    slot_of = routes[0].reshape(-1) * capacity + earlier
    slot_match = slot_of[:, None] == jnp.arange(slot_count, dtype=jnp.int32)[None, :]
    token_slots = jnp.sum(
        slot_match.reshape(tokens, fanout, slot_count).astype(jnp.int32), axis=1
    ).astype(jnp.bfloat16)
    outgoing = matmul_tn(token_slots, normed_mid).astype(jnp.bfloat16)
    doubled = jnp.repeat(outgoing.reshape(experts, capacity, width), 2, axis=0)
    expert_rows = lax.all_to_all(doubled, "ctx", split_axis=0, concat_axis=0, tiled=True).reshape(
        groups * capacity, width
    )
    halves = (
        lax.all_gather(w_gate, "fsdp", axis=2, tiled=True),
        lax.all_gather(w_up, "fsdp", axis=2, tiled=True),
        lax.all_gather(w_down, "fsdp", axis=1, tiled=True),
    )
    gate_full = halves[0][0]
    up_full = halves[1][0]
    down_full = halves[2][0]
    gate_pre = matmul(expert_rows, gate_full)
    up_pre = matmul(expert_rows, up_full)
    sigmoid_gate = jax.nn.sigmoid(gate_pre)
    activated = gate_pre * sigmoid_gate
    expert_hidden = (activated * up_pre).astype(jnp.bfloat16)
    expert_part = matmul(expert_hidden, down_full)
    returned_parts = lax.all_to_all(
        expert_part.reshape(groups, capacity, width).astype(jnp.bfloat16),
        "ctx",
        split_axis=0,
        concat_axis=0,
        tiled=True,
    ).astype(jnp.float32)
    returned = jnp.sum(returned_parts.reshape(experts, 2, capacity, width), axis=1).astype(
        jnp.bfloat16
    )
    returned = returned.reshape(slot_count, width)
    per_route = (
        jnp.take(returned, slot_of, axis=0).astype(jnp.float32).reshape(tokens, fanout, width)
    )
    layer_output = residual + jnp.sum(gates[:, :, None] * per_route, axis=1)
    query_back, key_back, value_back, output_back, router_back = (
        lax.all_gather(w_query, ("ctx", "fsdp"), axis=0, tiled=True),
        lax.all_gather(w_key, ("ctx", "fsdp"), axis=0, tiled=True),
        lax.all_gather(w_value, ("ctx", "fsdp"), axis=0, tiled=True),
        lax.all_gather(w_output, ("ctx", "fsdp"), axis=0, tiled=True),
        lax.all_gather(w_router, ("ctx", "fsdp"), axis=0, tiled=True),
    )
    grad_out = cotangent[0].astype(jnp.float32)
    grad_gate_w = jnp.sum(grad_out[:, None, :] * per_route, axis=-1)
    grad_probs = jnp.sum(jnp.where(chosen, grad_gate_w[:, :, None], 0.0), axis=1)
    grad_logits = router_probs * (
        grad_probs - jnp.sum(router_probs * grad_probs, axis=-1, keepdims=True)
    )
    grad_expert_out = (
        (gates[:, :, None] * grad_out[:, None, :])
        .astype(jnp.bfloat16)
        .reshape(tokens * fanout, width)
    )
    grad_outgoing = jnp.zeros((slot_count, width), jnp.bfloat16).at[slot_of].set(grad_expert_out)
    grad_doubled = jnp.repeat(grad_outgoing.reshape(experts, capacity, width), 2, axis=0)
    grad_rows = lax.all_to_all(
        grad_doubled, "ctx", split_axis=0, concat_axis=0, tiled=True
    ).reshape(groups * capacity, width)
    grad_hidden = matmul_nt(grad_rows, down_full)
    grad_gate_pre = (
        grad_hidden * up_pre * sigmoid_gate * (1.0 + gate_pre * (1.0 - sigmoid_gate))
    ).astype(jnp.bfloat16)
    grad_up_pre = (grad_hidden * activated).astype(jnp.bfloat16)
    grad_down_full = matmul_tn(expert_hidden, grad_rows)
    grad_gate_full = matmul_tn(expert_rows, grad_gate_pre)
    grad_up_full = matmul_tn(expert_rows, grad_up_pre)
    grad_expert_part = matmul_nt(grad_gate_pre, gate_full) + matmul_nt(grad_up_pre, up_full)
    expert_sums = (
        lax.psum_scatter(
            grad_gate_full[None].astype(jnp.bfloat16), "fsdp", scatter_dimension=2, tiled=True
        ).astype(jnp.float32),
        lax.psum_scatter(
            grad_up_full[None].astype(jnp.bfloat16), "fsdp", scatter_dimension=2, tiled=True
        ).astype(jnp.float32),
        lax.psum_scatter(
            grad_down_full[None].astype(jnp.bfloat16), "fsdp", scatter_dimension=1, tiled=True
        ).astype(jnp.float32),
    )
    grad_parts = lax.all_to_all(
        grad_expert_part.reshape(groups, capacity, width).astype(jnp.bfloat16),
        "ctx",
        split_axis=0,
        concat_axis=0,
        tiled=True,
    ).astype(jnp.float32)
    grad_returned = jnp.sum(grad_parts.reshape(experts, 2, capacity, width), axis=1).astype(
        jnp.bfloat16
    )
    grad_returned = grad_returned.reshape(slot_count, width)
    grad_mid = matmul(token_slots, grad_returned) + jnp.dot(
        grad_logits, router_back.astype(jnp.float32).T, precision=HIGH
    )
    grad_router_part = jnp.dot(normed_mid.astype(jnp.float32).T, grad_logits, precision=HIGH)
    grad_ffn_part = jnp.sum(grad_mid * normed_m, axis=0)
    grad_residual = grad_out + norm_back(grad_mid * ffn_gain, normed_m, factor_m)
    grad_branch = grad_residual.astype(jnp.bfloat16)
    grad_output_part = matmul_tn(attended, grad_branch)
    grad_attended = matmul_nt(grad_branch, output_back).astype(jnp.bfloat16)
    grad_att_groups = grad_attended.reshape(tokens, kv_heads, share, head_dim).transpose(1, 0, 2, 3)

    def query_side(query_part, key_part, value_part, total_part, grad_part):
        again = (
            jnp.einsum("qgd,kd->gqk", query_part, key_part, preferred_element_type=jnp.float32)
            * scale
        )
        probs = jnp.exp(again - total_part)
        grad_p = jnp.einsum(
            "qgd,kd->gqk", grad_part, value_part, preferred_element_type=jnp.float32
        )
        inner = jnp.sum(probs * grad_p, axis=-1, keepdims=True)
        grad_s = (probs * (grad_p - inner)).astype(jnp.bfloat16)
        grad_q = (
            jnp.einsum("gqk,kd->qgd", grad_s, key_part, preferred_element_type=jnp.float32) * scale
        )
        return (grad_q, grad_s, probs, inner)

    def backward_group(parts):
        grad_q, grad_s, probs, inner = query_side(*parts)
        return (grad_q, grad_s, probs.astype(jnp.bfloat16))

    grad_q_groups, grad_scores, weights_low = lax.map(
        backward_group, (query_groups, keys_heads, values_heads, log_totals, grad_att_groups)
    )
    key_part = (
        jnp.einsum("jgqk,jqgd->kjd", grad_scores, query_groups, preferred_element_type=jnp.float32)
        * scale
    )
    value_part = jnp.einsum(
        "jgqk,jqgd->kjd", weights_low, grad_att_groups, preferred_element_type=jnp.float32
    )
    key_value_sums = lax.psum_scatter(
        jnp.concatenate(
            [
                key_part.reshape(tokens * lax.axis_size("ctx"), kv_width),
                value_part.reshape(tokens * lax.axis_size("ctx"), kv_width),
            ],
            axis=1,
        ),
        "ctx",
        scatter_dimension=0,
        tiled=True,
    )
    grad_keys = key_value_sums[:, :kv_width].reshape(tokens, kv_heads, head_dim)
    grad_values = key_value_sums[:, kv_width:].astype(jnp.bfloat16)
    grad_queries = grad_q_groups.transpose(1, 0, 2, 3).reshape(tokens, heads, head_dim)
    grad_qn = rotate_back(grad_queries, cosine, sine)
    grad_kn = rotate_back(grad_keys, cosine, sine)
    grad_query_gain_part = jnp.sum(grad_qn * normed_q, axis=(0, 1))
    grad_key_gain_part = jnp.sum(grad_kn * normed_k, axis=(0, 1))
    grad_query_raw = (
        norm_back(grad_qn * query_gain, normed_q, factor_q)
        .reshape(tokens, width)
        .astype(jnp.bfloat16)
    )
    grad_key_raw = (
        norm_back(grad_kn * key_gain, normed_k, factor_k)
        .reshape(tokens, kv_width)
        .astype(jnp.bfloat16)
    )
    grad_query_part = matmul_tn(normed_in, grad_query_raw)
    grad_key_part = matmul_tn(normed_in, grad_key_raw)
    grad_value_part = matmul_tn(normed_in, grad_values)
    grad_normed_in = (
        matmul_nt(grad_query_raw, query_back)
        + matmul_nt(grad_key_raw, key_back)
        + matmul_nt(grad_values, value_back)
    )
    grad_attn_part = jnp.sum(grad_normed_in * normed_a, axis=0)
    grad_input = grad_residual + norm_back(grad_normed_in * attn_gain, normed_a, factor_a)
    summed = (
        lax.psum_scatter(grad_query_part, ("ctx", "fsdp"), scatter_dimension=0, tiled=True),
        lax.psum_scatter(grad_key_part, ("ctx", "fsdp"), scatter_dimension=0, tiled=True),
        lax.psum_scatter(grad_value_part, ("ctx", "fsdp"), scatter_dimension=0, tiled=True),
        lax.psum_scatter(grad_output_part, ("ctx", "fsdp"), scatter_dimension=0, tiled=True),
        lax.psum_scatter(grad_router_part, ("ctx", "fsdp"), scatter_dimension=0, tiled=True),
        lax.psum_scatter(grad_attn_part, ("ctx", "fsdp"), scatter_dimension=0, tiled=True),
        lax.psum_scatter(grad_ffn_part, ("ctx", "fsdp"), scatter_dimension=0, tiled=True),
    )
    gain_sums = lax.psum((grad_query_gain_part, grad_key_gain_part), ("ctx", "fsdp"))
    return (
        layer_output.astype(jnp.bfloat16)[None],
        grad_input[None],
        summed[5],
        summed[0],
        summed[1],
        summed[2],
        gain_sums[0],
        gain_sums[1],
        summed[3],
        summed[6],
        summed[4],
        expert_sums[0],
        expert_sums[1],
        expert_sums[2],
    )


def solution(mesh):
    placed = (
        P("fsdp", "ctx", None),
        P("fsdp", "ctx"),
        P("fsdp", "ctx", None),
        P(),
        P(("ctx", "fsdp"), None),
        P(("ctx", "fsdp"), None),
        P(("ctx", "fsdp"), None),
        P(),
        P(),
        P(("ctx", "fsdp"), None),
        P(),
        P(("ctx", "fsdp"), None),
        P("ctx", None, "fsdp"),
        P("ctx", None, "fsdp"),
        P("ctx", "fsdp", None),
        P("fsdp", "ctx", None),
    )
    return jax.shard_map(
        local,
        mesh=mesh,
        in_specs=placed,
        out_specs=(
            P("fsdp", "ctx", None),
            P("fsdp", "ctx", None),
            P(("ctx", "fsdp")),
            P(("ctx", "fsdp"), None),
            P(("ctx", "fsdp"), None),
            P(("ctx", "fsdp"), None),
            P(),
            P(),
            P(("ctx", "fsdp"), None),
            P(("ctx", "fsdp")),
            P(("ctx", "fsdp"), None),
            P("ctx", None, "fsdp"),
            P("ctx", None, "fsdp"),
            P("ctx", "fsdp", None),
        ),
        check_vma=False,
    )
```

profile of v0, /device:TPU:0, one launch (start us, length us, event | category | flops | bytes accessed | tf_op | source)
XLA Modules:
  0.0 5494.3 jit_solution(1015100958903343165)
XLA Ops:
  10.6 293.1 %all-gather.7.cloned.1.call-done = bf16[1024,512]{1,0:T(8,128)(2,1)} async-done(((bf16[8,512]{1,0:T(8,128)(2,1)}), bf16[1024,512]{1,0:T(8,128)(2,1)}) %all-gather.7.cloned.1.call-update) | async-done | bytes 1048592 | tf_op jit(solution)/shard_map/all_gather | solution.py:94
  306.9 290.8 %all-gather.11.cloned.1.call-done = bf16[1024,512]{1,0:T(8,128)(2,1)} async-done(((bf16[8,512]{1,0:T(8,128)(2,1)}), bf16[1024,512]{1,0:T(8,128)(2,1)}) %all-gather.11.cloned.1.call-update) | async-done | bytes 1048592 | tf_op jit(solution)/shard_map/all_gather | solution.py:93
  615.3 284.2 %all-gather.15.cloned.1.call-done = bf16[1024,1024]{1,0:T(8,128)(2,1)} async-done(((bf16[8,1024]{1,0:T(8,128)(2,1)}), bf16[1024,1024]{1,0:T(8,128)(2,1)}) %all-gather.15.cloned.1.call-update) | async-done | bytes 2097168 | tf_op jit(solution)/shard_map/all_gather | solution.py:92
  904.3 110.9 %all-gather.9.cloned.1.call-done = bf16[8192,512]{1,0:T(8,128)(2,1)} async-done(((bf16[128,512]{1,0:T(8,128)(2,1)}), bf16[8192,512]{1,0:T(8,128)(2,1)}) %all-gather.9.cloned.1.call-update) | async-done | bytes 8388624 | tf_op jit(solution)/shard_map/all_gather | solution.py:114
  1027.2 117.0 %all-gather.13.cloned.1.call-done = bf16[8192,512]{0,1:T(8,128)(2,1)} async-done(((bf16[128,512]{0,1:T(8,128)(2,1)}), bf16[8192,512]{0,1:T(8,128)(2,1)}) %all-gather.13.cloned.1.call-update) | async-done | bytes 8388624 | tf_op jit(solution)/shard_map/all_gather | solution.py:113
  1144.2 57.9 %while.28 = (s32[]{:T(128)}, bf16[8,128,2,64]{1,3,2,0:T(8,128)(2,1)S(1)}, f32[8,2,128,1]{2,1,3,0:T(2,128)}, bf16[8,8192,64]{1,2,0:T(8,128)(2,1)}, bf16[8,8192,64...) while((s32[]{:T(128)}, bf16[8,128,2,64]{1,3,2,0:T(8,128)(2,1)S(1)}, ...), condition=%wide.region_6.7_spmd.clone, body=%wide.region_3.6_spmd.sunk.clone | while | flops 551550720 | bytes 27371600 | solution.py:136
  1202.0 243.4 %all-gather.17.cloned.1.call-done = bf16[1024,1024]{1,0:T(8,128)(2,1)} async-done(((bf16[8,1024]{1,0:T(8,128)(2,1)}), bf16[1024,1024]{1,0:T(8,128)(2,1)}) %all-gather.17.cloned.1.call-update) | async-done | bytes 2097168 | tf_op jit(solution)/shard_map/all_gather | solution.py:95
  1462.3 78.8 %all_gather.42 = bf16[1,1024,256]{2,1,0:T(8,128)(2,1)S(1)} all-gather(bf16[1,1024,128]{2,1,0:T(8,128)(2,1)S(1)} %copy-done.46), channel_id=1, replica_groups=mesh['ctx'=64,'fsdp'=2] {'fsdp'}, dimensions={2}, use_global_device_ids=true | all-gather | bytes 786432 | tf_op jit(solution)/shard_map/all_gather | solution.py:160
  1579.0 19.0 all-to-all-start.1
  1598.3 386.6 %all_gather.41 = bf16[1024,32]{1,0:T(8,128)(2,1)S(1)} all-gather(bf16[8,32]{1,0:T(8,128)(2,1)S(1)} %copy-done.68), channel_id=1, replica_groups=mesh['ctx'=64,'fsdp'=2] {'ctx','fsdp'}, dimensions={0}, use_global_device_ids=true | all-gather | bytes 66048 | tf_op jit(solution)/shard_map/all_gather | solution.py:96
  2006.8 77.1 %all_to_all.20 = bf16[64,48,1024]{2,1,0:T(8,128)(2,1)S(1)} all-to-all(bf16[64,48,1024]{2,1,0:T(8,128)(2,1)S(1)} %bitcast.343), channel_id=1, replica_groups=mesh['ctx'=64,'fsdp'=2] {'ctx'}, dimensions={0} | all-to-all | bytes 12582912 | tf_op jit(solution)/shard_map/all_to_all | solution.py:208
  2106.6 79.2 %all-to-all-done.3 = bf16[64,48,1024]{2,1,0:T(8,128)(2,1)} async-done(((bf16[64,48,1024]{2,1,0:T(8,128)(2,1)}), bf16[64,48,1024]{2,1,0:T(8,128)(2,1)}, u32[]{:S(2)}, u32[]{:S(2)}) %all-to-all-start.3) | async-done | bytes 6291488 | tf_op jit(solution)/shard_map/all_to_all | solution.py:231
  2194.5 108.1 %while.29 = (s32[]{:T(128)}, f32[8,128,2,64]{1,3,2,0:T(8,128)}, bf16[8,2,128,8192]{2,3,1,0:T(8,128)(2,1)}, bf16[8,2,128,8192]{2,3,1,0:T(8,128)(2,1)}, bf16[8,819...) while((s32[]{:T(128)}, f32[8,128,2,64]{1,3,2,0:T(8,128)}, ...), condition=%wide.region_25.26_spmd.clone, body=%wide.region_23.25_spmd.sunk.clone | while | flops 822099712 | bytes 62005356 | solution.py:273
  2302.6 21.9 fusion.103
  2324.5 21.8 bitcast_multiply_fusion
  2346.4 23.6 pad_maximum_fusion
  2403.1 308.3 %reduce-scatter.13.cloned.1.call-done = f32[128,1024]{0,1:T(8,128)} async-done(((f32[8192,1024]{0,1:T(8,128)}), f32[128,1024]{0,1:T(8,128)}) %reduce-scatter.13.cloned.1.call-update) | async-done | bytes 524304 | tf_op jit(solution)/shard_map/reduce_scatter | solution.py:283
  2716.6 141.6 %all-reduce.6.cloned.1.call-done = f32[1024,32]{1,0:T(8,128)} async-done(((f32[1024,32]{1,0:T(8,128)}), f32[1024,32]{1,0:T(8,128)}) %all-reduce.6.cloned.1.call-update) | async-done | bytes 131088
  2859.4 19.6 reduce-scatter.25.cloned.1.call-done
  2925.2 66.7 %all-reduce.3 = (f32[1024]{0:T(1024)S(1)}, f32[64]{0:T(128)}, f32[64]{0:T(128)}, f32[1024]{0:T(1024)S(1)}) all-reduce(f32[1024]{0:T(1024)S(1)} %get-tuple-element.105, f32[64]{0:T(128)S(1)} %get-tuple-element.101, f32[64]{0:T(128)S(1)} %get-tuple-element.107, ...), channel_id=3, replica_groups=mesh['ctx'=64,'fsdp'=2] {'ctx','fsdp'}, use_global_device_ids=true, to_apply=%region_31.32.clone | all-reduce | flops 2176 | bytes 17408
  2994.1 573.8 %reduce-scatter.21.cloned.1.call-done = f32[8,1024]{1,0:T(8,128)} async-done(((f32[1024,1024]{1,0:T(8,128)}), f32[8,1024]{1,0:T(8,128)}) %reduce-scatter.21.cloned.1.call-update) | async-done | bytes 32784 | tf_op jit(solution)/shard_map/reduce_scatter | solution.py:326
  3567.9 642.7 %reduce-scatter.15.cloned.1.call-done = f32[8,1024]{1,0:T(8,128)} async-done(((f32[1024,1024]{1,0:T(8,128)}), f32[8,1024]{1,0:T(8,128)}) %reduce-scatter.15.cloned.1.call-update) | async-done | bytes 32784 | tf_op jit(solution)/shard_map/reduce_scatter | solution.py:323
  4210.6 637.8 %reduce-scatter.19.cloned.1.call-done = f32[8,512]{1,0:T(8,128)} async-done(((f32[1024,512]{1,0:T(8,128)}), f32[8,512]{1,0:T(8,128)}) %reduce-scatter.19.cloned.1.call-update) | async-done | bytes 16400 | tf_op jit(solution)/shard_map/reduce_scatter | solution.py:325
  4848.4 638.9 %reduce-scatter.17.cloned.1.call-done = f32[8,512]{1,0:T(8,128)} async-done(((f32[1024,512]{1,0:T(8,128)}), f32[8,512]{1,0:T(8,128)}) %reduce-scatter.17.cloned.1.call-update) | async-done | bytes 16400 | tf_op jit(solution)/shard_map/reduce_scatter | solution.py:324
  (370 shorter events, 401.5 us)
Async XLA Ops:
  7.2 594.2 %copy-start.64 = (f32[64]{0:T(128)S(1)}, f32[64]{0:T(128)}, u32[]{:S(2)}) copy-start(f32[64]{0:T(128)} %param.28) | copy-start | bytes 772
  7.2 595.6 %copy-start.56 = (s32[1,128,8]{1,2,0:T(8,128)S(1)}, s32[1,128,8]{1,2,0:T(8,128)}, u32[]{:S(2)}) copy-start(s32[1,128,8]{1,2,0:T(8,128)} %param.22) | copy-start | bytes 12292
  7.2 296.4 %all-gather.7.cloned.1.call-start = ((), (), s32[]{:S(2)}) async-start(), calls=%async_computation.12 | async-start | bytes 1056768 | tf_op jit(solution)/shard_map/all_gather | solution.py:94
  7.9 589.7 %all-gather.11.cloned.1.call-start = ((), (), s32[]{:S(2)}) async-start(), calls=%async_computation.14 | async-start | bytes 1056768 | tf_op jit(solution)/shard_map/all_gather | solution.py:93
  8.7 890.9 %all-gather.15.cloned.1.call-start = ((), (), s32[]{:S(2)}) async-start(), calls=%async_computation.16 | async-start | bytes 2113536 | tf_op jit(solution)/shard_map/all_gather | solution.py:92
  9.4 1005.8 %all-gather.9.cloned.1.call-start = ((), (), s32[]{:S(2)}) async-start(), calls=%async_computation.13 | async-start | bytes 8519680 | tf_op jit(solution)/shard_map/all_gather | solution.py:114
  10.6 891.9 %copy-start.57 = (f32[128]{0:T(128)}, f32[128]{0:T(128)S(1)}, u32[]{:S(2)}) copy-start(f32[128]{0:T(128)S(1)} %add_rsqrt_fusion.3) | copy-start | bytes 1540
  306.0 838.2 %all-gather.13.cloned.1.call-start = ((), (), s32[]{:S(2)}) async-start(), calls=%async_computation.15 | async-start | bytes 8519680 | tf_op jit(solution)/shard_map/all_gather | solution.py:113
  306.9 597.3 %copy-start.42 = (f32[128,32]{0,1:T(8,128)}, f32[128,32]{0,1:T(8,128)S(1)}, u32[]{:S(2)}) copy-start(f32[128,32]{0,1:T(8,128)S(1)} %get-tuple-element.166) | copy-start | bytes 49156
  306.9 597.3 %copy-start.44 = (f32[128,32]{0,1:T(8,128)}, f32[128,32]{0,1:T(8,128)S(1)}, u32[]{:S(2)}) copy-start(f32[128,32]{0,1:T(8,128)S(1)} %get-tuple-element.167) | copy-start | bytes 49156
  602.2 843.3 %all-gather.17.cloned.1.call-start = ((), (), s32[]{:S(2)}) async-start(), calls=%async_computation.17 | async-start | bytes 2113536 | tf_op jit(solution)/shard_map/all_gather | solution.py:95
  615.3 833.2 %copy-start.15 = (s32[128,1536]{1,0:T(8,128)}, s32[128,1536]{1,0:T(8,128)S(1)}, u32[]{:S(2)}) copy-start(s32[128,1536]{1,0:T(8,128)S(1)} %convert_reduce_fusion) | copy-start | bytes 2359300
  1453.1 107.9 %all-to-all-start = ((bf16[64,48,1024]{2,1,0:T(8,128)(2,1)}), bf16[64,48,1024]{2,1,0:T(8,128)(2,1)}, u32[]{:S(2)}, u32[]{:S(2)}) async-start(bf16[64,48,1024]{2,1,0:T(8,128)(2,1)} %bitcast.342), calls=%async_computation | async-start | bytes 12582912 | tf_op jit(solution)/shard_map/all_to_all | solution.py:156
  1579.0 407.2 %all-to-all-start.1 = ((bf16[64,48,1024]{2,1,0:T(8,128)(2,1)}), bf16[64,48,1024]{2,1,0:T(8,128)(2,1)}, u32[]{:S(2)}, u32[]{:S(2)}) async-start(bf16[64,48,1024]{2,1,0:T(8,128)(2,1)} %convolution_convert_fusion.1), calls=%async_computation.1 | async-start | bytes 12582912 | tf_op jit(solution)/shard_map/all_to_all | solution.py:173
  2093.4 92.3 %all-to-all-start.3 = ((bf16[64,48,1024]{2,1,0:T(8,128)(2,1)}), bf16[64,48,1024]{2,1,0:T(8,128)(2,1)}, u32[]{:S(2)}, u32[]{:S(2)}) async-start(bf16[64,48,1024]{2,1,0:T(8,128)(2,1)} %bitcast.344), calls=%async_computation.3 | async-start | bytes 12582912 | tf_op jit(solution)/shard_map/all_to_all | solution.py:231
  2104.5 606.9 %reduce-scatter.13.cloned.1.call-start = ((), (), s32[]{:S(2)}) async-start(), calls=%async_computation.18 | async-start | bytes 34078720 | tf_op jit(solution)/shard_map/reduce_scatter | solution.py:283
  2370.0 488.2 %all-reduce.6.cloned.1.call-start = ((), (), s32[]{:S(2)}) async-start(), calls=%async_computation.26 | async-start | bytes 1048576
  2372.1 506.9 %reduce-scatter.25.cloned.1.call-start = ((), (), s32[]{:S(2)}) async-start(), calls=%async_computation.24 | async-start | bytes 786432
  2381.2 518.0 %reduce-scatter.27.cloned.1.call-start = ((), (), s32[]{:S(2)}) async-start(), calls=%async_computation.25 | async-start | bytes 786432
  2390.7 529.2 %reduce-scatter.23.cloned.1.call-start = ((), (), s32[]{:S(2)}) async-start(), calls=%async_computation.23 | async-start | bytes 786432 | tf_op jit(solution)/shard_map/reduce_scatter | solution.py:227
  2396.5 1171.4 %reduce-scatter.21.cloned.1.call-start = ((), (), s32[]{:S(2)}) async-start(), calls=%async_computation.22 | async-start | bytes 4227072 | tf_op jit(solution)/shard_map/reduce_scatter | solution.py:326
  2399.3 1811.3 %reduce-scatter.15.cloned.1.call-start = ((), (), s32[]{:S(2)}) async-start(), calls=%async_computation.19 | async-start | bytes 4227072 | tf_op jit(solution)/shard_map/reduce_scatter | solution.py:323
  2403.1 2445.3 %reduce-scatter.19.cloned.1.call-start = ((), (), s32[]{:S(2)}) async-start(), calls=%async_computation.21 | async-start | bytes 2113536 | tf_op jit(solution)/shard_map/reduce_scatter | solution.py:325
  2714.3 2773.1 %reduce-scatter.17.cloned.1.call-start = ((), (), s32[]{:S(2)}) async-start(), calls=%async_computation.20 | async-start | bytes 2113536 | tf_op jit(solution)/shard_map/reduce_scatter | solution.py:324
  (67 other events, 4994.6 us)
Sparse Core Ops, SparseCore 0:
  9.7 293.8 all-gather.6
  305.3 292.2 all-gather.10
  599.4 300.1 all-gather.14
  901.7 113.4 all-gather.8
  1017.2 126.8 all-gather.12
  1145.7 299.7 all-gather.16
  2370.1 341.2 reduce-scatter.12
  2716.7 141.4 all-reduce.5
  2861.2 17.7 reduce-scatter.24
  2881.2 17.9 reduce-scatter.26
  2901.8 18.0 reduce-scatter.22
  2922.6 645.2 reduce-scatter.20
  3570.9 639.6 reduce-scatter.14
  4213.4 634.9 reduce-scatter.18
  4851.3 636.0 reduce-scatter.16
where the time goes:
time: 5510 us; the launch traced here: 5490 us
  waiting for transfers between devices  4420 us (80%)
  blocking collectives  629 us (11%)
  matrix products  226 us (4%)
  other arithmetic  112 us (2%)
    reduce_scatter x1, waiting for transfers between devices, local(): lax.psum_scatter(grad_query_part, ('ctx', 'fsdp'), scatter_dimension=0, t...  643 us
    reduce_scatter x1, waiting for transfers between devices, local(): lax.psum_scatter(grad_key_part, ('ctx', 'fsdp'), scatter_dimension=0, til...  639 us
    reduce_scatter x1, waiting for transfers between devices, local(): lax.psum_scatter(grad_value_part, ('ctx', 'fsdp'), scatter_dimension=0, t...  638 us
    reduce_scatter x1, waiting for transfers between devices, local(): lax.psum_scatter(grad_output_part, ('ctx', 'fsdp'), scatter_dimension=0,...  574 us
    all_gather x1, blocking collectives, local(): lax.all_gather(w_router, ('ctx', 'fsdp'), axis=0, tiled=True)  387 us
    reduce_scatter x1, waiting for transfers between devices, local(): lax.psum_scatter(jnp.concatenate([key_part.reshape(tokens * lax.axis_size...  308 us
    all_gather x1, waiting for transfers between devices, local(): lax.all_gather(w_value, ('ctx', 'fsdp'), axis=0, tiled=True)  293 us
    all_gather x1, waiting for transfers between devices, local(): lax.all_gather(w_key, ('ctx', 'fsdp'), axis=0, tiled=True)  291 us
  transfers between devices with their start and end apart: 18, of which 16 were waited for; matrix products, arithmetic and copies ran while one was open for 3% of the time, Pallas kernels for 0%

commit v1 on v0

v1 whole, which is shorter than its diff:
```python
import functools

import jax
import jax.numpy as jnp
from jax import lax
from jax.experimental import pallas as pl
from jax.experimental.pallas import tpu as pltpu
from jax.sharding import PartitionSpec as P

EPS = 1e-06
LOG2E = 1.4426950408889634
LN2 = 0.6931471805599453
MESH = pl.DeviceIdType.MESH
BF = jnp.bfloat16
F32 = jnp.float32
NT = (((1,), (1,)), ((), ()))
TN = (((0,), (0,)), ((), ()))
HBM = pl.BlockSpec(memory_space=pl.ANY)
VMEM = pl.BlockSpec(memory_space=pltpu.VMEM)
DMA = pltpu.SemaphoreType.DMA
STEPS = ((0, 0), (0, 1), (0, 3), (1, 0), (1, 1), (1, 3), (0, 2), (1, 2))


def dot(left, right, dims=(((1,), (0,)), ((), ()))):
    return lax.dot_general(left, right, dims, preferred_element_type=F32)


class Place:
    def __init__(self):
        ctx = lax.axis_index("ctx")
        self.f = lax.axis_index("fsdp")
        self.t = lax.rem(ctx, 8)
        self.g = lax.div(ctx, 8)
        self.core = lax.rem(ctx, 2)
        self.z = lax.rem(lax.div(ctx, 2), 4)
        self.y = lax.rem(self.g, 4)
        self.xl = lax.div(self.g, 4)
        self.chip = lax.div(ctx, 2)

    def tp(self, k):
        t = lax.rem(self.t + k, 8)
        return t, (self.g * 8 + t, self.f)

    def cp(self, k, back=False):
        a, b = STEPS[k]
        xl = lax.rem(self.xl + a, 2)
        y = lax.rem(self.y + (4 - b if back else b), 4)
        g = xl * 4 + y
        return g, (g * 8 + self.t, self.f)

    def gf(self, k):
        r = lax.rem(self.g * 2 + self.f + k, 16)
        return r, (lax.div(r, 2) * 8 + self.t, lax.rem(r, 2))

    def chips(self, k):
        a, b, c = k // 16, (k // 4) % 4, k % 4
        xl = lax.rem(self.xl + a, 2)
        y = lax.rem(self.y + b, 4)
        z = lax.rem(self.z + c, 4)
        e = (xl * 4 + y) * 4 + z
        return e, (e * 2 + self.core, self.f)

    def zpeer(self, c):
        z = lax.rem(self.z + c, 4)
        t = z * 2 + self.core
        return z, t, (self.g * 8 + t, self.f)

    def sibling(self):
        t = self.z * 2 + 1 - self.core
        return t, (self.g * 8 + t, self.f)

    def partner(self):
        return (self.g * 8 + self.t, 1 - self.f)


def greet(devices):
    sem = pltpu.get_barrier_semaphore()
    for d in devices:
        pl.semaphore_signal(sem, inc=1, device_id=d, device_id_type=MESH)
    return sem


def send(src, dst, send_sem, recv_sem, device):
    copy = pltpu.make_async_remote_copy(
        src_ref=src,
        dst_ref=dst,
        send_sem=send_sem,
        recv_sem=recv_sem,
        device_id=device,
        device_id_type=MESH,
    )
    copy.start()
    return copy


def local_copy(src, dst, sem):
    copy = pltpu.make_async_copy(src, dst, sem)
    copy.start()
    return copy


def landed(ref, sem):
    pltpu.make_async_copy(ref, ref, sem).wait()


def chips_all(p, src, dst, sends, recv):
    copies = []
    for k in range(1, 32):
        e, dev = p.chips(k)
        copies.append(send(src.at[e], dst.at[p.chip], sends.at[k], recv, dev))
    copies.append(local_copy(src.at[p.chip], dst.at[p.chip], sends.at[0]))
    return copies


def chips_done(copies, dst, recv):
    landed(dst.at[pl.ds(0, 31)], recv)
    for c in copies[:-1]:
        c.wait_send()
    copies[-1].wait()


def start_kernel(x, wp, pos, xg, wg, posg, wst, xs, xr, fs, fr, ps, pr, ws, wr, gs, gr, ls):
    p = Place()
    sem = greet([p.tp(k)[1] for k in range(1, 8)] + [p.gf(k)[1] for k in range(1, 16)])
    pl.semaphore_wait(sem, 22)
    tsib, sib = p.sibling()
    outs = []
    zs = []
    for c in (1, 3, 2):
        _, _, dev = p.zpeer(c)
        zs.append(send(x, xg.at[p.t], xs.at[c], xr.at[c], dev))
    for k in range(1, 8):
        t, dev = p.tp(k)
        outs.append(send(wp.at[t], wst.at[p.t], ws.at[k], wr, dev))
    outs.append(send(x, xg.at[p.t], xs.at[0], xr.at[0], sib))
    for k in range(1, 8):
        t, dev = p.tp(k)
        outs.append(send(pos, posg.at[p.t], ps.at[k], pr, dev))
    own = [
        local_copy(x, xg.at[p.t], ls.at[0]),
        local_copy(pos, posg.at[p.t], ls.at[1]),
        local_copy(wp.at[p.t], wst.at[p.t], ls.at[2]),
    ]
    own[2].wait()
    landed(wst.at[pl.ds(0, 7)], wr)
    me = p.g * 2 + p.f
    own.append(local_copy(wst, wg.at[me], ls.at[3]))
    for k in range(1, 16):
        _, dev = p.gf(k)
        outs.append(send(wst, wg.at[me], gs.at[k], gr, dev))
    fwd = []
    for c in (1, 3, 2):
        landed(xg.at[0], xr.at[c])
        z = lax.rem(p.z + 4 - c, 4)
        block = xg.at[z * 2 + p.core]
        fwd.append(send(block, block, fs.at[c], fr.at[c], sib))
    landed(posg.at[pl.ds(0, 7)], pr)
    landed(wg.at[pl.ds(0, 15)], gr)
    landed(xg.at[0], xr.at[0])
    for c in (1, 3, 2):
        landed(xg.at[0], fr.at[c])
    for c in zs + outs + fwd:
        c.wait_send()
    for c in (own[0], own[1], own[3]):
        c.wait()


def start(x, wp, pos):
    return pl.pallas_call(
        start_kernel,
        out_shape=(
            jax.ShapeDtypeStruct((8, 128, 1024), BF),
            jax.ShapeDtypeStruct((16, 8, 16, 128), BF),
            jax.ShapeDtypeStruct((8, 8, 128), F32),
        ),
        in_specs=[HBM] * 3,
        out_specs=(HBM,) * 3,
        scratch_shapes=[
            pltpu.VMEM((8, 16, 128), BF),
            DMA((4,)),
            DMA((4,)),
            DMA((4,)),
            DMA((4,)),
            DMA((8,)),
            DMA,
            DMA((8,)),
            DMA,
            DMA((16,)),
            DMA,
            DMA((4,)),
        ],
        compiler_params=pltpu.CompilerParams(collective_id=0, has_side_effects=True),
        name="start",
    )(x, wp, pos)


QB = 256


def forward_kernel(
    qp,
    kv,
    cot,
    eg,
    eu,
    ed,
    wop,
    attg,
    o,
    lse,
    kvall,
    cotr,
    egr,
    eur,
    edr,
    wog,
    att,
    acc,
    lsum,
    wst,
    ks,
    kr,
    as_,
    ar,
    cs,
    cr,
    es,
    er,
    fs,
    fr,
    ws,
    wr,
    gs,
    gr,
    ls,
):
    p = Place()
    tsib, sib = p.sibling()
    sem = greet(
        [p.chips(k)[1] for k in range(1, 32)]
        + [p.tp(k)[1] for k in range(1, 8)]
        + [p.gf(k)[1] for k in range(1, 16)]
    )
    pl.semaphore_wait(sem, 31 + 7 + 15)
    outs = []
    for k in range(1, 8):
        _, dev = p.cp(k)
        outs.append(send(kv, kvall.at[k], ks.at[k], kr.at[k], dev))
    own_kv = local_copy(kv, kvall.at[0], kr.at[0])
    for k in range(1, 8):
        _, dev = p.tp(k)
        outs.append(send(wop, wst.at[p.t], ws.at[k], wr, dev))
    own_wo = local_copy(wop, wst.at[p.t], ls.at[0])
    mine = p.core * 2 + p.f
    other = p.core * 2 + 1 - p.f
    own_e = []
    pieces = ((eg, egr), (eu, eur), (ed, edr))
    for i, (src, dst) in enumerate(pieces):
        outs.append(send(src, dst.at[mine], es.at[i], er.at[i], p.partner()))
        outs.append(send(src, dst.at[mine], es.at[3 + i], er.at[3 + i], sib))
        own_e.append(local_copy(src, dst.at[mine], ls.at[1 + i]))
    cots = chips_all(p, cot, cotr, cs, cr)

    acc[...] = jnp.zeros_like(acc)
    lsum[...] = jnp.zeros_like(lsum)

    def slot(k, _):
        landed(kvall.at[0], kr.at[k])
        kvb = kvall[k]

        def block(i, _):
            rows = pl.ds(pl.multiple_of(i * QB, QB), QB)
            s = dot(qp[rows, :], kvb, NT)
            e = jnp.exp2(s)
            part = e[:, 0:128]
            for j in range(1, 8):
                part = part + e[:, j * 128 : (j + 1) * 128]
            lsum[rows, :] += part
            acc[rows, :] += dot(e.astype(BF), kvb)
            return 0

        lax.fori_loop(0, 2048 // QB, block, 0)
        return 0

    lax.fori_loop(0, 2, slot, 0)
    own_wo.wait()
    landed(wst.at[pl.ds(0, 7)], wr)
    me = p.g * 2 + p.f
    own_wg = local_copy(wst, wog.at[me], ls.at[4])
    for k in range(1, 16):
        _, dev = p.gf(k)
        outs.append(send(wst, wog.at[me], gs.at[k], gr, dev))
    lax.fori_loop(2, 6, slot, 0)
    for i, (_, dst) in enumerate(pieces):
        landed(dst.at[0], er.at[i])
        outs.append(send(dst.at[other], dst.at[other], fs.at[i], fr.at[i], sib))
    lax.fori_loop(6, 8, slot, 0)

    lane = lax.broadcasted_iota(jnp.int32, (128, 128), 1)
    ones = jnp.ones((8, 128), F32)
    for t in range(8):
        parts = []
        for h in range(2):
            rows = pl.ds(h * 1024 + t * 128, 128)
            total = jnp.sum(lsum[rows, :], axis=1, keepdims=True)
            parts.append(acc[rows, :] / total)
        whole = jnp.where(lane < 64, pltpu.roll(parts[0], 64, 1), parts[1])
        o[pl.ds(t * 128, 128), :] = whole
        att[t] = whole.astype(BF)
    for k in range(1, 8):
        t, dev = p.tp(k)
        outs.append(send(att.at[t], attg.at[p.t], as_.at[k], ar, dev))
    own_att = local_copy(att.at[p.t], attg.at[p.t], ls.at[5])
    for h in range(2):
        rows = lax.dot_general(
            ones,
            lsum[pl.ds(h * 1024, 1024), :],
            NT,
            precision=lax.Precision.HIGHEST,
            preferred_element_type=F32,
        )
        lse[h] = jnp.log2(rows)

    landed(attg.at[pl.ds(0, 7)], ar)
    landed(wog.at[pl.ds(0, 15)], gr)
    for i, (_, dst) in enumerate(pieces):
        landed(dst.at[0], er.at[3 + i])
        landed(dst.at[0], fr.at[i])
    chips_done(cots, cotr, cr)
    for c in outs:
        c.wait_send()
    for c in own_e + [own_wg, own_att]:
        c.wait()


def forward(qp, kv, cot, eg, eu, ed, wop):
    return pl.pallas_call(
        forward_kernel,
        out_shape=(
            jax.ShapeDtypeStruct((8, 128, 128), BF),
            jax.ShapeDtypeStruct((1024, 128), F32),
            jax.ShapeDtypeStruct((2, 8, 1024), F32),
            jax.ShapeDtypeStruct((8, 1024, 128), BF),
            jax.ShapeDtypeStruct((32, 48, 1024), BF),
            jax.ShapeDtypeStruct((4, 1024, 128), BF),
            jax.ShapeDtypeStruct((4, 1024, 128), BF),
            jax.ShapeDtypeStruct((4, 128, 1024), BF),
            jax.ShapeDtypeStruct((16, 8, 80, 128), BF),
        ),
        in_specs=[VMEM, HBM, HBM, HBM, HBM, HBM, HBM],
        out_specs=(HBM, VMEM, VMEM, VMEM, HBM, HBM, HBM, HBM, HBM),
        scratch_shapes=[
            pltpu.VMEM((8, 128, 128), BF),
            pltpu.VMEM((2048, 128), F32),
            pltpu.VMEM((2048, 128), F32),
            pltpu.VMEM((8, 80, 128), BF),
            DMA((8,)),
            DMA((8,)),
            DMA((8,)),
            DMA,
            DMA((32,)),
            DMA,
            DMA((6,)),
            DMA((6,)),
            DMA((3,)),
            DMA((3,)),
            DMA((8,)),
            DMA,
            DMA((16,)),
            DMA,
            DMA((6,)),
        ],
        compiler_params=pltpu.CompilerParams(
            collective_id=1, has_side_effects=True, vmem_limit_bytes=48 * 2**20
        ),
        name="attention_forward",
    )(qp, kv, cot, eg, eu, ed, wop)


def rows_kernel(src, dst, ss, rs):
    p = Place()
    sem = greet([p.chips(k)[1] for k in range(1, 32)])
    pl.semaphore_wait(sem, 31)
    chips_done(chips_all(p, src, dst, ss, rs), dst, rs)


def rows_out(src, number, name):
    return pl.pallas_call(
        rows_kernel,
        out_shape=jax.ShapeDtypeStruct(src.shape, src.dtype),
        in_specs=[HBM],
        out_specs=HBM,
        scratch_shapes=[DMA((32,)), DMA],
        compiler_params=pltpu.CompilerParams(collective_id=number, has_side_effects=True),
        name=name,
    )(src)


KB = 256
GB = 512


def backward_kernel(
    qp,
    kvall,
    o,
    lse,
    gat,
    gb,
    ysend,
    dw,
    dqt,
    dkv,
    gbg,
    yret,
    dwr,
    gatr,
    dop,
    delta,
    acc,
    dks,
    dkr,
    as_,
    ar,
    bs,
    br,
    ys,
    yr,
    es,
    er,
    ss,
    sr,
    ls,
):
    p = Place()
    tsib, sib = p.sibling()
    sem = greet(
        [p.chips(k)[1] for k in range(1, 32)]
        + [p.tp(k)[1] for k in range(1, 8)]
        + [p.partner(), (p.g * 8 + tsib, 1 - p.f)]
    )
    pl.semaphore_wait(sem, 31 + 7 + 2)
    outs = []
    for k in range(1, 8):
        t, dev = p.tp(k)
        outs.append(send(gat.at[t], gatr.at[p.t], as_.at[k], ar, dev))
    own = [local_copy(gat.at[p.t], gatr.at[p.t], ls.at[0])]
    own[0].wait()
    landed(gatr.at[pl.ds(0, 7)], ar)
    for k in range(1, 8):
        _, dev = p.tp(k)
        outs.append(send(gb, gbg.at[p.t], bs.at[k], br, dev))
    own_gb = local_copy(gb, gbg.at[p.t], ls.at[1])
    mine = p.core * 2 + p.f
    owners = (
        (p.core * 2 + 1 - p.f, p.partner()),
        ((1 - p.core) * 2 + p.f, sib),
        ((1 - p.core) * 2 + 1 - p.f, (p.g * 8 + tsib, 1 - p.f)),
    )
    for i, (q, dev) in enumerate(owners):
        outs.append(send(dw.at[q], dwr.at[1 + i], es.at[i], er.at[i], dev))
    own_dw = local_copy(dw.at[mine], dwr.at[0], ls.at[2])
    yrows = chips_all(p, ysend, yret, ys, yr)

    lane = lax.broadcasted_iota(jnp.int32, (128, 128), 1)
    ones = jnp.ones((8, 128), F32)
    for t in range(8):
        both = gatr[t].astype(F32)
        rows = pl.ds(t * 128, 128)
        first = jnp.where(lane < 64, 0.0, pltpu.roll(both, 64, 1))
        second = jnp.where(lane < 64, 0.0, both)
        dop[rows, :] = first.astype(BF)
        dop[pl.ds(1024 + t * 128, 128), :] = second.astype(BF)
        prod = both * o[rows, :]
        for h in range(2):
            part = jnp.where((lane < 64) == (h == 0), prod, 0.0)
            delta[h, :, rows] = lax.dot_general(
                ones, part, NT, precision=lax.Precision.HIGHEST, preferred_element_type=F32
            )
    dqt[...] = jnp.zeros_like(dqt)

    def slot(s, carry):
        def keys(j, _):
            krows = pl.ds(pl.multiple_of(j * KB, KB), KB)
            kvb = kvall[s, krows, :]
            kt = kvb.T[:64, :]
            total = jnp.zeros((KB, 128), F32)
            for i in range(2048 // GB):
                rows = pl.ds(i * GB, GB)
                h, cols = i * GB // 1024, pl.ds(i * GB % 1024, GB)
                q = qp[rows, :]
                d = dop[rows, :]
                w = jnp.exp2(dot(kvb, q, NT) - lse[h, 0:1, cols])
                ds = (w * (dot(kvb, d, NT) - delta[h, 0:1, cols])).astype(BF)
                total = total + dot(w.astype(BF), d) + dot(ds, q)
                dqt[:, rows] += dot(kt, ds)
            acc[krows, :] = total
            return 0

        lax.fori_loop(0, 1024 // KB, keys, 0)

    for k in (7, 6, 5, 4, 3, 2, 1):
        slot(k, 0)
        dks[k] = acc[...].astype(BF)
        _, dev = p.cp(k, back=True)
        outs.append(send(dks.at[k], dkr.at[k], ss.at[k], sr.at[k], dev))
    slot(0, 0)
    whole = acc[...]
    for k in range(1, 8):
        landed(dkr.at[0], sr.at[k])
        whole = whole + dkr[k].astype(F32)
    dkv[...] = whole

    landed(gbg.at[pl.ds(0, 7)], br)
    for i in range(3):
        landed(dwr.at[0], er.at[i])
    chips_done(yrows, yret, yr)
    for c in outs:
        c.wait_send()
    own_gb.wait()
    own_dw.wait()


def backward(qp, kvall, o, lse, gat, gb, ysend, dw):
    return pl.pallas_call(
        backward_kernel,
        out_shape=(
            jax.ShapeDtypeStruct((64, 2048), F32),
            jax.ShapeDtypeStruct((1024, 128), F32),
            jax.ShapeDtypeStruct((8, 128, 1024), BF),
            jax.ShapeDtypeStruct((32, 48, 1024), BF),
            jax.ShapeDtypeStruct(dw.shape, BF),
        ),
        in_specs=[VMEM, VMEM, VMEM, VMEM, HBM, HBM, HBM, HBM],
        out_specs=(VMEM, VMEM, HBM, HBM, HBM),
        scratch_shapes=[
            pltpu.VMEM((8, 128, 128), BF),
            pltpu.VMEM((2048, 128), BF),
            pltpu.VMEM((2, 8, 1024), F32),
            pltpu.VMEM((1024, 128), F32),
            pltpu.VMEM((8, 1024, 128), BF),
            pltpu.VMEM((8, 1024, 128), BF),
            DMA((8,)),
            DMA,
            DMA((8,)),
            DMA,
            DMA((32,)),
            DMA,
            DMA((3,)),
            DMA((3,)),
            DMA((8,)),
            DMA((8,)),
            DMA((3,)),
        ],
        compiler_params=pltpu.CompilerParams(
            collective_id=4, has_side_effects=True, vmem_limit_bytes=56 * 2**20
        ),
        name="attention_backward",
    )(qp, kvall, o, lse, gat, gb, ysend, dw)


def final_kernel(
    dx,
    dwm,
    dwo,
    dxs,
    d2r,
    dwor,
    sibr,
    zsend,
    zr,
    dwr,
    d2s,
    d2l,
    ss,
    sr,
    zs,
    zrs,
    ws,
    wrs,
    ts,
    trs,
    os_,
    ors,
    ls,
):
    p = Place()
    tsib, sib = p.sibling()
    sem = greet([p.tp(k)[1] for k in range(1, 8)] + [p.gf(k)[1] for k in range(1, 16)])
    self_in = p.g == p.t
    for q in range(8):
        for f in range(2):
            to = (q * 8 + p.g, f)

            @pl.when(jnp.logical_not(jnp.logical_and(self_in, jnp.logical_and(q == p.g, f == p.f))))
            def _():
                pl.semaphore_signal(sem, inc=1, device_id=to, device_id_type=MESH)

    pl.semaphore_wait(sem, 7 + 15 + 16 - jnp.where(self_in, 1, 0))
    outs = []
    for c in (1, 2, 3, 0):
        z = lax.rem(p.z + c, 4)
        outs.append(send(dx.at[1 - p.core, z], sibr.at[z], ss.at[c], sr.at[c], sib))
    me = p.g * 2 + p.f
    for k in range(1, 16):
        r, dev = p.gf(k)
        outs.append(send(dwm.at[r], dwr.at[me], ws.at[k], wrs, dev))
    own_dw = local_copy(dwm.at[me], dwr.at[me], ls.at[0])
    for q in range(8):
        for f in range(2):
            to = (p.t * 8 + q, f)
            is_self = jnp.logical_and(self_in, jnp.logical_and(q == p.t, f == p.f))
            src, dst = dwo.at[q * 2 + f], dwor.at[p.g * 2 + p.f]

            @pl.when(jnp.logical_not(is_self))
            def _():
                send(src, dst, os_.at[q * 2 + f], ors.at[p.g * 2 + p.f], to)

            @pl.when(is_self)
            def _():
                local_copy(src, dst, ls.at[1])

    for c in (1, 3, 2):
        z, _, dev = p.zpeer(c)
        landed(sibr.at[0], sr.at[c])
        zsend[c] = (dx[p.core, z].astype(F32) + sibr[z].astype(F32)).astype(BF)
        outs.append(send(zsend.at[c], zr.at[c], zs.at[c], zrs.at[c], dev))
    landed(sibr.at[0], sr.at[0])
    whole = dx[p.core, p.z].astype(F32) + sibr[p.z].astype(F32)

    own_dw.wait()
    landed(dwr.at[pl.ds(0, 15)], wrs)
    total = dwr[0].astype(F32)
    for r in range(1, 16):
        total = total + dwr[r].astype(F32)
    for t in range(8):
        d2s[t, 0:8, :] = total[t * 8 : (t + 1) * 8, :]
        d2s[t, 8:16, :] = total[64:72, :]
    for k in range(1, 8):
        t, dev = p.tp(k)
        outs.append(send(d2s.at[t], d2l.at[p.t], ts.at[k], trs, dev))
    own_d2 = local_copy(d2s.at[p.t], d2l.at[p.t], ls.at[2])
    for c in (1, 3, 2):
        landed(zr.at[0], zrs.at[c])
        whole = whole + zr[c].astype(F32)
    dxs[...] = whole
    for q in range(8):
        for f in range(2):
            is_self = jnp.logical_and(self_in, jnp.logical_and(q == p.t, f == p.f))
            src, dst = dwo.at[q * 2 + f], dwor.at[p.g * 2 + p.f]

            @pl.when(jnp.logical_not(is_self))
            def _():
                landed(src, os_.at[q * 2 + f])

            @pl.when(is_self)
            def _():
                landed(dst, ls.at[1])

            from_self = jnp.logical_and(self_in, jnp.logical_and(q == p.g, f == p.f))

            @pl.when(jnp.logical_not(from_self))
            def _():
                landed(dwor.at[0], ors.at[q * 2 + f])

    own_d2.wait()
    landed(d2l.at[pl.ds(0, 7)], trs)
    d2r[...] = d2l[...]
    for c in outs:
        c.wait_send()


def final(dx, dwm, dwo):
    return pl.pallas_call(
        final_kernel,
        out_shape=(
            jax.ShapeDtypeStruct((128, 1024), F32),
            jax.ShapeDtypeStruct((8, 16, 384), F32),
            jax.ShapeDtypeStruct((16, 8, 1024), F32),
        ),
        in_specs=[VMEM, HBM, HBM],
        out_specs=(VMEM, VMEM, HBM),
        scratch_shapes=[
            pltpu.VMEM((4, 128, 1024), BF),
            pltpu.VMEM((4, 128, 1024), BF),
            pltpu.VMEM((4, 128, 1024), BF),
            pltpu.VMEM((16, 80, 384), BF),
            pltpu.VMEM((8, 16, 384), F32),
            pltpu.VMEM((8, 16, 384), F32),
            DMA((4,)),
            DMA((4,)),
            DMA((4,)),
            DMA((4,)),
            DMA((16,)),
            DMA,
            DMA((8,)),
            DMA,
            DMA((16,)),
            DMA((16,)),
            DMA((3,)),
        ],
        compiler_params=pltpu.CompilerParams(
            collective_id=5, has_side_effects=True, vmem_limit_bytes=32 * 2**20
        ),
        name="last_sums",
    )(dx, dwm, dwo)


def norm_stats(v):
    factor = lax.rsqrt(jnp.mean(v * v, axis=-1, keepdims=True) + EPS)
    return v * factor, factor


def norm_back(grad_normed, normed, factor):
    return factor * (grad_normed - normed * jnp.mean(grad_normed * normed, axis=-1, keepdims=True))


def rotate(v, cosine, sine):
    first, second = jnp.split(v, 2, axis=-1)
    return jnp.concatenate(
        [first * cosine - second * sine, second * cosine + first * sine], axis=-1
    )


def local(
    layer_input,
    positions,
    routes,
    attn_gain,
    w_query,
    w_key,
    w_value,
    query_gain,
    key_gain,
    w_output,
    ffn_gain,
    w_router,
    w_gate,
    w_up,
    w_down,
    cotangent,
):
    x = layer_input[0]
    cot = cotangent[0]
    expert = lax.div(lax.axis_index("ctx"), 2)

    wq = w_query.reshape(8, 8, 128).transpose(1, 0, 2)
    wk = w_key.reshape(8, 8, 64).transpose(1, 0, 2)
    wv = w_value.reshape(8, 8, 64).transpose(1, 0, 2)
    wp = jnp.concatenate([wq, jnp.concatenate([wk, wv], axis=2)], axis=1)
    pos = jnp.broadcast_to(positions.astype(F32), (8, 128))
    xg, wg, posg = start(x, wp, pos)

    experts = jnp.arange(32, dtype=jnp.int32)
    chosen = routes[0][:, :, None] == experts[None, None, :]
    hits = jnp.sum(chosen.astype(F32), axis=1)
    earlier = dot(jnp.tril(jnp.ones((128, 128), BF), -1), hits.astype(BF))
    place = jnp.where(hits > 0, earlier, -1.0)
    token_slots = (
        (place[:, :, None] == jnp.arange(48, dtype=F32)[None, None, :])
        .astype(BF)
        .reshape(128, 32 * 48)
    )
    cot_out = dot(token_slots, cot, TN).astype(BF).reshape(32, 48, 1024)

    xf = xg.reshape(1024, 1024).astype(F32)
    normed_a, factor_a = norm_stats(xf)
    normed_in = (normed_a * attn_gain).astype(BF)
    wqkv = (
        wg.reshape(8, 2, 8, 2, 8, 128).transpose(0, 2, 1, 4, 3, 5).reshape(1024, 256)
    )
    raw = dot(normed_in, wqkv)
    steps = jnp.arange(32, dtype=F32) * (2.0 / 64)
    inverse = jnp.power(50000.0, -steps)
    angles = posg[:, 0, :].reshape(1024, 1) * inverse
    cosine, sine = jnp.cos(angles), jnp.sin(angles)
    normed_q, factor_q = norm_stats(raw[:, :128].reshape(1024, 2, 64))
    normed_k, factor_k = norm_stats(raw[:, 128:192])
    scale = 0.125 * LOG2E
    queries = (rotate(normed_q * query_gain, cosine[:, None], sine[:, None]) * scale).astype(BF)
    keys = rotate(normed_k * key_gain, cosine, sine).astype(BF)
    values = raw[:, 192:].astype(BF)
    kv = jnp.concatenate([keys, values], axis=1)
    qp = jnp.pad(queries.transpose(1, 0, 2), ((0, 0), (0, 0), (0, 64))).reshape(2048, 128)

    wop = jnp.concatenate(
        [w_output.reshape(64, 128), jnp.pad(w_router, ((0, 8), (0, 96)))], axis=0
    )
    attg, o, lse, kvall, cot_rows, egr, eur, edr, wog = forward(
        qp, kv, cot_out, w_gate[0], w_up[0], w_down[0], wop
    )

    wog = wog.reshape(8, 2, 8, 80, 128).transpose(0, 2, 1, 3, 4)
    wo = wog[:, :, :, :64].reshape(1024, 1024)
    wr = wog[:, :, :, 64:72, :32].reshape(1024, 32)
    attended = attg.transpose(1, 0, 2).reshape(128, 1024)
    residual = x.astype(F32) + dot(attended, wo)
    normed_m, factor_m = norm_stats(residual)
    normed_mid = (normed_m * ffn_gain).astype(BF)
    outgoing = dot(token_slots, normed_mid, TN).astype(BF).reshape(32, 48, 1024)
    rows = rows_out(outgoing, 2, "rows_out").reshape(1536, 1024)

    grads = cot_rows.reshape(1536, 1024)
    gate_w = egr.transpose(1, 0, 2).reshape(1024, 512)
    up_w = eur.transpose(1, 0, 2).reshape(1024, 512)
    down_w = edr.reshape(512, 1024)
    grad_hidden0 = dot(grads, down_w, NT)
    gate_pre = dot(rows, gate_w)
    up_pre = dot(rows, up_w)
    logits = dot(rows, wr)
    expo = jnp.exp(logits - jnp.max(logits, axis=1, keepdims=True))
    probs = expo / jnp.sum(expo, axis=1, keepdims=True)
    here = (experts == expert).astype(F32)[None, :]
    gate = jnp.sum(probs * here, axis=1, keepdims=True)
    sig = jax.nn.sigmoid(gate_pre)
    activated = gate_pre * sig
    hidden = activated * up_pre
    grad_gate_w = jnp.sum(hidden * grad_hidden0, axis=1, keepdims=True)
    gated_hidden = (gate * hidden).astype(BF)
    grad_hidden = gate * grad_hidden0
    grad_gate_pre = (grad_hidden * up_pre * sig * (1.0 + gate_pre * (1.0 - sig))).astype(BF)
    grad_up_pre = (grad_hidden * activated).astype(BF)
    grad_logits = (grad_gate_w * gate * (here - probs)).astype(BF)
    grad_in = (
        dot(grad_gate_pre, gate_w, NT) + dot(grad_up_pre, up_w, NT) + dot(grad_logits, wr, NT)
    ).astype(BF)
    back = rows_out(grad_in.reshape(32, 48, 1024), 3, "rows_back").reshape(1536, 1024)
    mixed = dot(gated_hidden, down_w).astype(BF).reshape(32, 48, 1024)
    grad_gate = dot(rows, grad_gate_pre, TN).astype(BF).reshape(1024, 4, 128).transpose(1, 0, 2)
    grad_up = dot(rows, grad_up_pre, TN).astype(BF).reshape(1024, 4, 128).transpose(1, 0, 2)
    grad_down = dot(gated_hidden, grads, TN).astype(BF).reshape(4, 1024, 128)
    dw = jnp.stack([grad_gate, grad_up, grad_down], axis=1)
    grad_router = dot(rows, grad_logits, TN)

    grad_out = cot.astype(F32)
    grad_mid = dot(token_slots, back)
    grad_ffn = jnp.sum(grad_mid * normed_m, axis=0)
    grad_residual = grad_out + norm_back(grad_mid * ffn_gain, normed_m, factor_m)
    grad_branch = grad_residual.astype(BF)
    grad_attended = dot(grad_branch, wo, NT).astype(BF)
    gat = grad_attended.reshape(128, 8, 128).transpose(1, 0, 2)
    dqt, dkv, gbg, yret, dwr = backward(qp, kvall, o, lse, gat, grad_branch, mixed, dw)

    layer_output = residual + dot(token_slots, yret.reshape(1536, 1024))
    dws = jnp.sum(dwr.astype(F32), axis=0)

    dq = dqt.reshape(64, 2, 1024).transpose(2, 1, 0) * 0.125
    dk = dkv[:, :64] * LN2
    dqn = rotate(dq, cosine[:, None], -sine[:, None])
    dkn = rotate(dk, cosine, -sine)
    query_gain_part = jnp.sum(dqn * normed_q, axis=(0, 1))
    key_gain_part = jnp.sum(dkn * normed_k, axis=0)
    dq_raw = norm_back(dqn * query_gain, normed_q, factor_q).reshape(1024, 128)
    dk_raw = norm_back(dkn * key_gain, normed_k, factor_k)
    draw = jnp.concatenate([dq_raw, dk_raw, dkv[:, 64:]], axis=1).astype(BF)
    dwqkv = dot(normed_in, draw, TN)
    dx = dot(draw, wqkv, NT)
    attn_part = jnp.sum(dx * normed_a, axis=0)
    att_t = o.astype(BF)
    dwo = dot(att_t, gbg.reshape(1024, 1024), TN).reshape(16, 8, 1024)

    misc = jnp.concatenate(
        [grad_router, grad_ffn[:, None], attn_part[:, None], jnp.zeros((1024, 94), F32)], axis=1
    )
    both = jnp.concatenate([dwqkv, misc], axis=1).astype(BF)
    both = both.reshape(8, 8, 2, 8, 384).transpose(0, 2, 1, 3, 4).reshape(16, 64, 384)
    gains = jnp.concatenate([query_gain_part, key_gain_part, jnp.zeros((256,), F32)])
    gains = jnp.broadcast_to(gains.astype(BF), (16, 16, 384))
    dwm = jnp.concatenate([both, gains], axis=1)
    dxp = dx.astype(BF).reshape(4, 2, 128, 1024).transpose(1, 0, 2, 3)
    dxs, d2, dwor = final(dxp, dwm, dwo)

    normed_own, factor_own = norm_stats(x.astype(F32))
    grad_input = grad_residual + norm_back(dxs * attn_gain, normed_own, factor_own)
    own = d2[:, :8].transpose(1, 0, 2)
    sums = jnp.sum(own[:, :, 256:], axis=1)
    gain_sums = jnp.sum(d2[:, 8, :128], axis=0)
    return (
        layer_output.astype(BF)[None],
        grad_input[None],
        sums[:, 33],
        own[:, :, :128].reshape(8, 1024),
        own[:, :, 128:192].reshape(8, 512),
        own[:, :, 192:256].reshape(8, 512),
        gain_sums[:64],
        gain_sums[64:],
        jnp.sum(dwor, axis=0),
        sums[:, 32],
        sums[:, :32],
        dws[0][None],
        dws[1][None],
        dws[2].reshape(1, 128, 1024),
    )


def solution(mesh):
    rows = P(("ctx", "fsdp"), None)
    vector = P(("ctx", "fsdp"))
    tokens = P("fsdp", "ctx", None)
    return jax.shard_map(
        local,
        mesh=mesh,
        in_specs=(
            tokens,
            P("fsdp", "ctx"),
            tokens,
            P(),
            rows,
            rows,
            rows,
            P(),
            P(),
            rows,
            P(),
            rows,
            P("ctx", None, "fsdp"),
            P("ctx", None, "fsdp"),
            P("ctx", "fsdp", None),
            tokens,
        ),
        out_specs=(
            tokens,
            tokens,
            vector,
            rows,
            rows,
            rows,
            P(),
            P(),
            rows,
            vector,
            rows,
            P("ctx", None, "fsdp"),
            P("ctx", None, "fsdp"),
            P("ctx", "fsdp", None),
        ),
        check_vma=False,
    )
```

time: 5510 us -> 547 us (0.10)
  waiting for transfers between devices: 4420 us -> 0 us
  blocking collectives: 629 us -> 0 us
  Pallas kernels: 0 us -> 390 us
  matrix products: 226 us -> 58.3 us
  other arithmetic: 112 us -> 35.2 us
    reduce_scatter x6 -> x0, waiting for transfers between devices: 2820 us -> none  [the longest x1 643 us: local(): lax.psum_scatter(grad_query_part, ('ctx', 'fsdp'), scatter_dimension=0, t...]
    all_gather x6 -> x0, waiting for transfers between devices: 1340 us -> none  [the longest x1 293 us: local(): lax.all_gather(w_value, ('ctx', 'fsdp'), axis=0, tiled=True)]
    all_gather x4 -> x0, blocking collectives: 485 us -> none  [the longest x1 387 us: local(): lax.all_gather(w_router, ('ctx', 'fsdp'), axis=0, tiled=True)]
    pallas_call x0 -> x6, Pallas kernels: none -> 390 us  [the longest x1 121 us: forward(): pl.pallas_call(forward_kernel, out_shape=(jax.ShapeDtypeStruct((8, 128, 1...]
    unnamed x18 -> x0, waiting for transfers between devices: 182 us -> none
    dot_general x68 -> x23, matrix products: 226 us -> 58.3 us  [dot(): return lax.dot_general(left, right, dims, preferred_element_type=F32)]
    all_to_all x3 -> x0, waiting for transfers between devices: 79.2 us -> none  [the longest x1 79.2 us: local(): lax.all_to_all(grad_expert_part.reshape(groups, capacity, width).astype(j...]
    all_to_all x1 -> x0, blocking collectives: 77.1 us -> none  [local(): lax.all_to_all(grad_doubled, 'ctx', split_axis=0, concat_axis=0, tiled=True)]
  transfers between devices with their start and end apart: 18 -> 0, of which waited for: 16 -> 0; matrix products, arithmetic and copies ran while one was open for 3% -> 0% of each run, Pallas kernels for 0% -> 0%
where the time goes in v1:
time: 547 us; the launch traced here: 539 us
  Pallas kernels  390 us (71%)
  matrix products  58.3 us (11%)
  local copies, waits for them, and re-layouts  53.2 us (10%)
  other arithmetic  35.2 us (6%)
    pallas_call x1, Pallas kernels, forward(): pl.pallas_call(forward_kernel, out_shape=(jax.ShapeDtypeStruct((8, 128, 1...  121 us
    pallas_call x1, Pallas kernels, backward(): pl.pallas_call(backward_kernel, out_shape=(jax.ShapeDtypeStruct((64, 2048...  107 us
    pallas_call x2, Pallas kernels, rows_out(): pl.pallas_call(rows_kernel, out_shape=jax.ShapeDtypeStruct(src.shape, src...  91.2 us
    dot_general x23, matrix products, dot(): return lax.dot_general(left, right, dims, preferred_element_type=F32)  58.3 us
    pallas_call x1, Pallas kernels, final(): pl.pallas_call(final_kernel, out_shape=(jax.ShapeDtypeStruct((128, 1024),...  39.6 us
    pallas_call x1, Pallas kernels, start(): pl.pallas_call(start_kernel, out_shape=(jax.ShapeDtypeStruct((8, 128, 102...  31.5 us

profile of v1, /device:TPU:0, one launch (start us, length us, event | category | flops | bytes accessed | tf_op | source)
XLA Modules:
  0.0 538.5 jit_solution(9857950888254926657)
XLA Ops:
  10.3 31.5 %start.1 = (bf16[8,128,1024]{2,1,0:T(8,128)(2,1)}, bf16[16,8,16,128]{3,2,1,0:T(8,128)(2,1)}, f32[8,8,128]{2,1,0:T(8,128)}) custom-call(bf16[128,1024]{1,0:T(8,128)(2,1)} %bitcast.208, bf16[8,16,128]{2,1,0:T(8,128)(2,1)} %maximum_maximum_fusion.wp, f32[8,128]{1,0:T(8,128)} %broadcast_in_dim.25.pos), custom_call_target="tpu_custom_call" | custom-call | tf_op jit(solution)/shard_map/start/pallas_call | solution.py:169
  49.0 3.3 fusion.11
  56.7 120.5 %attention_forward.1 = (bf16[8,128,128]{2,1,0:T(8,128)(2,1)S(1)}, f32[1024,128]{1,0:T(8,128)S(1)}, f32[2,8,1024]{2,1,0:T(8,128)S(1)}, bf16[8,1024,128]{2,1,0:T(8...) custom-call(bf16[2048,128]{1,0:T(8,128)(2,1)S(1)} %bitcast.185, ...), custom_call_target="tpu_custom_call" | custom-call | tf_op jit(solution)/shard_map/attention_forward/pallas_call | solution.py:337
  183.5 4.2 reshape.373
  193.4 2.7 convolution_convert_fusion.1
  196.1 46.8 %rows_out.1 = bf16[32,48,1024]{2,1,0:T(8,128)(2,1)} custom-call(bf16[32,48,1024]{2,1,0:T(8,128)(2,1)} %bitcast.202), custom_call_target="tpu_custom_call" | custom-call | tf_op jit(solution)/shard_map/rows_out/pallas_call | solution.py:388
  242.9 3.1 fusion.59
  246.2 3.4 copy.126
  249.6 3.2 fusion.62
  255.1 4.9 multiply_reduce_fusion.2
  264.6 5.3 convolution_convert_fusion.4
  269.9 2.8 convolution_convert_fusion.3
  276.8 3.3 pad_maximum_fusion.dw
  280.2 3.5 convolution_convert_fusion
  287.4 2.8 add_convert_fusion
  290.2 44.4 %rows_back.1 = bf16[32,48,1024]{2,1,0:T(8,128)(2,1)} custom-call(bf16[32,48,1024]{2,1,0:T(8,128)(2,1)} %bitcast.201), custom_call_target="tpu_custom_call" | custom-call | tf_op jit(solution)/shard_map/rows_back/pallas_call | solution.py:388
  334.6 2.8 multiply_reduce_fusion.5
  341.4 107.1 %attention_backward.1 = (f32[64,2048]{1,0:T(8,128)}, f32[1024,128]{1,0:T(8,128)}, bf16[8,128,1024]{2,1,0:T(8,128)(2,1)}, bf16[32,48,1024]{2,1,0:T(8,128)(2,1)}, bf16[4,3,1024,128]{3,2,1,0:T(8,128)(2,1)}) custom-call(bf16[2048,128]{1,0:T(8,128)(2,1)} %bitcast.186, bf16[8,1024,128]{2,1,0:T(8,128)(2,1)} %get-tuple-element.39.kvall, f32[1024,128]{1,0:T(8,128)} %copy-done.1, ...), custom_call_target="tpu_custom_call" | custom-call | tf_op jit(solution)/shard_map/attention_backward/pallas_call | solution.py:525
  448.6 3.4 fusion.3
  466.5 4.5 multiply_reduce_fusion
  476.9 4.0 copy.124
  480.9 3.1 convolution_convert_fusion.6
  484.7 3.1 concatenate.57
  489.0 39.6 %last_sums.1 = (f32[128,1024]{1,0:T(8,128)S(1)}, f32[8,16,384]{2,1,0:T(8,128)S(1)}, f32[16,8,1024]{2,1,0:T(8,128)S(1)}) custom-call(bf16[2,4,128,1024]{3,2,1,0:T(8,128)(2,1)S(1)} %bitcast.184, bf16[16,80,384]{2,1,0:T(8,128)(2,1)S(1)} %pad_maximum_fusion.2.dwm, f32[16,8,1024]{2,1,0:T(8,128)S(1)} %fusion.33.dwo), custom_call_target="tpu_custom_call" | custom-call | tf_op jit(solution)/shard_map/last_sums/pallas_call | solution.py:674
  (224 shorter events, 83.1 us)
Async XLA Ops:
  0.6 45.3 %copy-start.44 = (f32[1024]{0:T(1024)S(1)}, f32[1024]{0:T(1024)}, u32[]{:S(2)}) copy-start(f32[1024]{0:T(1024)} %param.19) | copy-start | bytes 12292
  41.8 4.1 copy-start.21
  48.7 4.0 copy-start.17
  53.2 3.6 copy-start.4
  53.6 123.7 %copy-start = (bf16[2,1024,128]{2,1,0:T(8,128)(2,1)}, bf16[2,1024,128]{2,1,0:T(8,128)(2,1)S(1)}, u32[]{:S(2)}) copy-start(bf16[2,1024,128]{2,1,0:T(8,128)(2,1)S(1)} %pad.8) | copy-start | bytes 1572868
  178.9 8.8 %copy-start.1 = (f32[1024,128]{1,0:T(8,128)}, f32[1024,128]{1,0:T(8,128)S(1)}, u32[]{:S(2)}) copy-start(f32[1024,128]{1,0:T(8,128)S(1)} %get-tuple-element.40.o) | copy-start | bytes 1572868
  183.5 5.1 copy-start.22
  188.5 4.8 copy-start.39
  188.5 4.8 copy-start.42
  190.7 5.4 %copy-start.13 = (f32[128,1024]{1,0:T(8,128)}, f32[128,1024]{1,0:T(8,128)S(1)}, u32[]{:S(2)}) copy-start(f32[128,1024]{1,0:T(8,128)S(1)} %get-tuple-element.96) | copy-start | bytes 1572868
  264.6 5.3 copy-start.11
  264.6 5.3 copy-start.51
  290.2 44.4 %copy-start.14 = (f32[128,1024]{1,0:T(8,128)S(1)}, f32[128,1024]{1,0:T(8,128)}, u32[]{:S(2)}) copy-start(f32[128,1024]{1,0:T(8,128)} %copy-done.13) | copy-start | bytes 1572868
  334.6 4.0 copy-start.29
  334.6 5.0 copy-start.12
  337.4 111.1 %copy-start.25 = (f32[128,1024]{1,0:T(8,128)}, f32[128,1024]{1,0:T(8,128)S(1)}, u32[]{:S(2)}) copy-start(f32[128,1024]{1,0:T(8,128)S(1)} %get-tuple-element.99) | copy-start | bytes 1572868
  337.4 111.1 %copy-start.47 = (f32[128]{0:T(128)}, f32[128]{0:T(128)S(1)}, u32[]{:S(2)}) copy-start(f32[128]{0:T(128)S(1)} %broadcast_multiply_fusion.4) | copy-start | bytes 1540
  448.6 3.9 copy-start.34
  452.0 3.7 copy-start.16
  455.7 5.1 copy-start.24
  462.2 4.2 copy-start.32
  476.0 4.8 copy-start.40
  476.9 4.0 copy-start.41
  487.9 44.3 %copy-start.48 = (f32[128]{0:T(128)S(1)}, f32[128]{0:T(128)}, u32[]{:S(2)}) copy-start(f32[128]{0:T(128)} %copy-done.47) | copy-start | bytes 1540
  (31 other events, 69.8 us)
